TPU v7x, 32 devices: a whole 2x2x4 slice. The times are simulated.
32 devices in a mesh: angle: 4 (over y, core), tile: 8 (over z, x).
Axes of the slice: x: 2, y: 2, z: 4, core: 2. Of those that a mesh axis runs over, the one named last changes fastest.
Arguments:
- patches: bfloat16 [4, 64, 2, 128, 128], P('angle', 'tile'), may hold values from -6 to 6
- magnitudes: bfloat16 [4, 128, 128, 128], P('angle', 'tile'), may hold values from 0.099609375 to 3
- probe: float32 [2, 128, 128], replicated, may hold values from -6 to 6
- owners: int32 [4, 64, 1], P('angle', 'tile'), may hold values from 0 to 7; in each aligned block of 8 rows (0 to 7, 8 to 15, ..., all dimensions but the last counted through in order) at most 2 rows name the same one
- scan_rows: int32 [4, 64], P('angle', 'tile'), may hold values from 0 to 384
- scan_cols: int32 [4, 64], P('angle', 'tile'), may hold values from 0 to 896
- slab_rows: int32 [8, 4], P('tile'), may hold values from 0 to 32, as said below
- angle_tan: float32 [4], replicated, may hold values from -0.4 to 0.4
- prior_in: bfloat16 [16, 1, 3, 3], replicated, may hold values from -2 to 2
- prior_out: bfloat16 [1, 16, 3, 3], replicated, may hold values from -0.5 to 0.5
Outputs:
- volume: float32 [8, 128, 16, 1024], P('tile', 'angle')
Inputs may be any that keep to these rules, and one draw needn't show every extreme that they name: `owners`: in the patches of one device, no owner is named by more than 2, and in some devices one owner is named exactly 2 times. Each row of slab_rows sums to 64, and in every row some slab has exactly 32 rows.
All inputs are finite; a program needn't handle non-finite values.
Results may differ from a plain program's by a relative error of at most 0.022.
Values may be sent and summed in bfloat16 or wider, within the bound.
No kernel may reach another device: no remote copies, remote signals or barrier semaphores. Data moves between devices by JAX's collectives and lax.ppermute only.
A program may use at most 128 MiB of HBM per device.

v0:
```python
import math

import jax
import jax.numpy as jnp
from jax import lax
from jax.sharding import PartitionSpec as P

H = 512
W = 1024
XW = 16


def dft_table(side):
    index = jnp.arange(side, dtype=jnp.int32)
    product = index[:, None] * index[None, :] % side
    phase = product.astype(jnp.float32) * (2.0 * math.pi / side)
    scale = 1.0 / math.sqrt(side)
    real = jnp.cos(phase) * scale
    imag = -jnp.sin(phase) * scale
    upper = jnp.concatenate([real, imag], axis=1)
    lower = jnp.concatenate([-imag, real], axis=1)
    return jnp.concatenate([upper, lower], axis=0).astype(jnp.bfloat16)


def correct_all(waves, measured, table):
    number = waves.shape[0]
    side = waves.shape[2]
    left = table.T
    joined = jnp.concatenate([waves[:, 0], waves[:, 1]], axis=2).reshape(number * side, 2 * side)
    half = jnp.dot(joined, table, preferred_element_type=jnp.float32).astype(jnp.bfloat16)
    half = half.reshape(number, side, 2 * side)
    stacked = jnp.concatenate([half[:, :, :side], half[:, :, side:]], axis=1)
    stacked = jnp.transpose(stacked, (1, 0, 2)).reshape(2 * side, number * side)
    spectrum = jnp.dot(left, stacked, preferred_element_type=jnp.float32).reshape(
        2 * side, number, side
    )
    real_part = spectrum[:side]
    imag_part = spectrum[side:]
    level = jnp.transpose(measured, (1, 0, 2)).astype(jnp.float32)
    factor = level / jnp.sqrt(real_part * real_part + imag_part * imag_part + 0.25)
    target = jnp.concatenate([real_part * factor, imag_part * factor], axis=2).astype(jnp.bfloat16)
    back = jnp.dot(
        target.reshape(side * number, 2 * side), left, preferred_element_type=jnp.float32
    )
    back = back.astype(jnp.bfloat16).reshape(side, number, 2 * side)
    stacked_back = jnp.concatenate([back[:, :, :side], back[:, :, side:]], axis=0).reshape(
        2 * side, number * side
    )
    result = jnp.dot(table, stacked_back, preferred_element_type=jnp.float32).reshape(
        2, side, number, side
    )
    return jnp.transpose(result, (2, 0, 1, 3)).astype(jnp.bfloat16)


def backproject(sino, angle_tan, width):
    count = sino.shape[1]
    offsets = jnp.arange(XW, dtype=jnp.float32) - (XW - 1) / 2.0
    spread_cols = int(0.2 * (XW - 1)) + 2
    shifts = jnp.arange(-spread_cols, spread_cols + 1, dtype=jnp.int32).astype(jnp.float32)

    def add_angle(total, item):
        rows, tangent = item
        shifted = offsets * tangent
        floor_shift = jnp.floor(shifted)
        fraction = shifted - floor_shift
        low_hit = (shifts[None, :] == floor_shift[:, None]).astype(jnp.float32)
        high_hit = (shifts[None, :] == floor_shift[:, None] + 1.0).astype(jnp.float32)
        weights = (1.0 - fraction)[:, None] * low_hit + fraction[:, None] * high_hit
        padded = jnp.pad(rows, ((0, 0), (spread_cols, spread_cols)))
        columns_stack = jnp.stack(
            [padded[:, step : step + width] for step in range(2 * spread_cols + 1)], axis=0
        )
        term = jnp.einsum("is,scj->cij", weights, columns_stack, precision=lax.Precision.HIGHEST)
        return (total + term, None)

    start = jnp.zeros((count, XW, width), jnp.float32)
    total, unused = lax.scan(add_angle, start, (sino, angle_tan))
    return total / sino.shape[0]


def prior(slices, prior_in, prior_out):
    numbers = ("NCHW", "OIHW", "NCHW")
    rounded = slices.astype(jnp.bfloat16)[:, None].astype(jnp.float32)
    hidden = lax.conv_general_dilated(
        rounded, prior_in.astype(jnp.float32), (1, 1), "SAME", dimension_numbers=numbers
    )
    hidden = jnp.maximum(hidden, 0.0).astype(jnp.bfloat16).astype(jnp.float32)
    extra = lax.conv_general_dilated(
        hidden, prior_out.astype(jnp.float32), (1, 1), "SAME", dimension_numbers=numbers
    )
    return slices + extra[:, 0]


def body(
    patches,
    magnitudes,
    probe,
    owners,
    scan_rows,
    scan_cols,
    slab_rows,
    angle_tan,
    prior_in,
    prior_out,
):
    tiles = lax.axis_size("tile")
    angles = lax.axis_size("angle")
    count = patches.shape[1]
    side = patches.shape[3]
    slots = magnitudes.shape[1]
    depth = slots // tiles
    table = dft_table(side)
    owner = owners[0, :, 0]
    member = (owner[:, None] == jnp.arange(tiles, dtype=jnp.int32)[None, :]).astype(jnp.int32)
    before = jnp.sum((jnp.cumsum(member, axis=0) - member) * member, axis=1)
    slot = owner * depth + before
    select = (jnp.arange(slots, dtype=jnp.int32)[:, None] == slot[None, :]).astype(jnp.bfloat16)
    waves = patches[0]
    packed = jnp.dot(select, waves.reshape(count, -1), preferred_element_type=jnp.float32).astype(
        jnp.bfloat16
    )
    arrived = lax.all_to_all(
        packed.reshape(tiles, depth, 2, side, side), "tile", split_axis=0, concat_axis=0, tiled=True
    )
    fixed = correct_all(arrived.reshape(slots, 2, side, side), magnitudes[0], table)
    returned = lax.all_to_all(
        fixed.reshape(tiles, depth, 2, side, side), "tile", split_axis=0, concat_axis=0, tiled=True
    )
    mine = jnp.dot(select.T, returned.reshape(slots, -1), preferred_element_type=jnp.float32)
    mine = mine.astype(jnp.bfloat16).reshape(count, 2, side, side)
    mine_float = mine.astype(jnp.float32)
    contrib = (probe[0] * mine_float[:, 1] - probe[1] * mine_float[:, 0]) * 0.25
    rows_here = scan_rows[0]
    cols_here = scan_cols[0]
    width = W

    def place(step, canvas):
        row = rows_here[step]
        col = cols_here[step]
        piece = lax.dynamic_slice(canvas, (row, col), (side, side)) + contrib[step]
        return lax.dynamic_update_slice(canvas, piece, (row, col))

    canvas = lax.fori_loop(0, count, place, jnp.zeros((H, width), jnp.float32))
    strip = lax.psum_scatter(
        canvas.astype(jnp.bfloat16), "tile", scatter_dimension=0, tiled=True
    ).astype(jnp.float32)
    strip_rows = strip.shape[0]
    rowcap = 2 * strip_rows // angles
    lengths = slab_rows[0]
    starts = jnp.cumsum(lengths) - lengths
    within = jnp.arange(rowcap, dtype=jnp.int32)
    index = jnp.clip(starts[:, None] + within[None, :], 0, strip_rows - 1)
    valid = (within[None, :] < lengths[:, None]).astype(jnp.float32)
    outgoing = strip[index] * valid[:, :, None]
    slabs = prior(
        backproject(
            lax.all_to_all(
                outgoing.astype(jnp.bfloat16), "angle", split_axis=0, concat_axis=0, tiled=True
            ).astype(outgoing.dtype),
            angle_tan,
            width,
        ),
        prior_in,
        prior_out,
    )
    return slabs[None]


def solution(mesh):
    placed = (
        P("angle", "tile", None, None, None),
        P("angle", "tile", None, None),
        P(),
        P("angle", "tile", None),
        P("angle", "tile"),
        P("angle", "tile"),
        P("tile", None),
        P(),
        P(),
        P(),
    )
    return jax.shard_map(
        body, mesh=mesh, in_specs=placed, out_specs=P("tile", "angle", None, None), check_vma=False
    )
```

profile of v0, /device:TPU:0, one launch (start us, length us, event | category | flops | bytes accessed | tf_op | source)
XLA Modules:
  0.0 443.6 jit_solution(3854325924631668000)
XLA Ops:
  8.8 1.3 reshape_squeeze.3
  11.7 7.3 %all-to-all-start = ((bf16[8,2,2,128,128]{4,3,2,1,0:T(8,128)(2,1)}), bf16[8,2,2,128,128]{4,3,2,1,0:T(8,128)(2,1)S(1)}, u32[]{:S(2)}, u32[]{:S(2)}) async-start(bf16[8,2,2,128,128]{4,3,2,1,0:T(8,128)(2,1)} %bitcast.64), calls=%async_computation | async-start | bytes 2097152 | tf_op jit(solution)/shard_map/all_to_all | solution.py:122
  19.5 25.2 %all-to-all-done = bf16[8,2,2,128,128]{4,3,2,1,0:T(8,128)(2,1)S(1)} async-done(((bf16[8,2,2,128,128]{4,3,2,1,0:T(8,128)(2,1)}), bf16[8,2,2,128,128]{4,3,2,1,0:T(8,128)(2,1)S(1)}, u32[]{:S(2)}, u32[]{:S(2)}) %all-to-all-start) | async-done | bytes 1048608 | tf_op jit(solution)/shard_map/all_to_all | solution.py:122
  51.7 3.6 all-to-all-start.1
  55.4 25.9 %all-to-all-done.1 = bf16[8,2,2,128,128]{4,3,2,1,0:T(8,128)(2,1)S(1)} async-done(((bf16[8,2,2,128,128]{4,3,2,1,0:T(8,128)(2,1)}), bf16[8,2,2,128,128]{4,3,2,1,0:T(8,128)(2,1)S(1)}, u32[]{:S(2)}, u32[]{:S(2)}) %all-to-all-start.1) | async-done | bytes 1048608 | tf_op jit(solution)/shard_map/all_to_all | solution.py:126
  82.8 57.2 %while.27 = (s32[]{:T(128)}, f32[512,1024]{1,0:T(8,128)S(1)}, s32[8]{0:T(128)S(1)}, s32[8]{0:T(128)S(1)}, f32[8,128,128]{2,1,0:T(8,128)S(1)}, /*index=5*/s32[]{:T(128)}, s32[]{:T(128)}, s32[]{:T(128)}, s32[]{:T(128)}) while((s32[]{:T(128)}, f32[512,1024]{1,0:T(8,128)S(1)}, s32[8]{0:T(128)S(1)}, s32[8]{0:T(128)S(1)}, ...), condition=%wide.region_3.4_spmd, body=%wide.region_2.3_spmd.sunk | while | flops 16392 | bytes 327889 | solution.py:143
  88.0 2.0 dynamic_update_slice.8
  95.2 1.9 dynamic_update_slice.8
  102.3 2.0 dynamic_update_slice.8
  109.6 2.0 dynamic_update_slice.8
  116.8 2.0 dynamic_update_slice.8
  124.0 2.0 dynamic_update_slice.8
  131.2 1.7 dynamic_update_slice.8
  138.1 1.9 dynamic_update_slice.8
  141.7 62.9 %reduce-scatter.2.cloned.1.call-done = bf16[64,1024]{1,0:T(8,128)(2,1)} async-done(((bf16[512,1024]{1,0:T(8,128)(2,1)}), bf16[64,1024]{1,0:T(8,128)(2,1)}) %reduce-scatter.2.cloned.1.call-update) | async-done | bytes 131088 | tf_op jit(solution)/shard_map/reduce_scatter | solution.py:144
  207.1 3.6 all-to-all-start.2
  210.7 5.8 %all-to-all-done.2 = bf16[4,32,1024]{2,1,0:T(8,128)(2,1)S(1)} async-done(((bf16[4,32,1024]{2,1,0:T(8,128)(2,1)}), bf16[4,32,1024]{2,1,0:T(8,128)(2,1)S(1)}, u32[]{:S(2)}, u32[]{:S(2)}) %all-to-all-start.2) | async-done | bytes 262176 | tf_op jit(solution)/shard_map/all_to_all | solution.py:157
  216.6 48.8 %while.28 = (s32[]{:T(128)}, f32[32,16,1024]{2,1,0:T(8,128)}, f32[4,32,1024]{2,1,0:T(8,128)S(1)}, f32[4]{0:T(128)S(1)}, s32[]{:T(128)}, /*index=5*/s32[]{:T(128)}, f32[4]{0:T(128)}) while((s32[]{:T(128)}, f32[32,16,1024]{2,1,0:T(8,128)}, f32[4,32,1024]{2,1,0:T(8,128)S(1)}, f32[4]{0:T(128)S(1)}, s32[]{:T(128)}, ...), condition=%wide.region_7.8_spmd.clone.clone, body=%wide.region_6.7_spmd.clone.clone.sunk | while | flops 70255656 | bytes 17564520 | solution.py:77
  221.3 2.3 stack.92
  223.6 4.5 %bitcast_add_fusion.5 = f32[32,16,1024]{2,1,0:T(8,128)} fusion(f32[32,16,1024]{2,1,0:T(8,128)} %get-tuple-element.390, f32[11,32,1024]{2,0,1:T(8,128)S(1)} %stack.92, pred[]{:T(512)S(6)} %compare.5, f32[16]{0:T(128)} %get-tuple-element.352, f32[16]{0:T(128)S(1)} %get-tuple-element.353, f32[11]{0:T(128)S(1)} %add_convert_fusion.2, ...), kind=kOutput, calls=%fused_computation.4.clone.1 | convolution fusion | flops 70255472 | bytes 5636397 | tf_op jit(solution)/shard_map/while/body/eval_jaxpr/is,scj->cij/dot_general | solution.py:73
  232.8 2.3 stack.92
  235.1 5.4 %bitcast_add_fusion.5 = f32[32,16,1024]{2,1,0:T(8,128)} fusion(f32[32,16,1024]{2,1,0:T(8,128)} %get-tuple-element.390, f32[11,32,1024]{2,0,1:T(8,128)S(1)} %stack.92, pred[]{:T(512)S(6)} %compare.5, f32[16]{0:T(128)} %get-tuple-element.352, f32[16]{0:T(128)S(1)} %get-tuple-element.353, f32[11]{0:T(128)S(1)} %add_convert_fusion.2, ...), kind=kOutput, calls=%fused_computation.4.clone.1 | convolution fusion | flops 70255472 | bytes 5636397 | tf_op jit(solution)/shard_map/while/body/eval_jaxpr/is,scj->cij/dot_general | solution.py:73
  245.2 2.3 stack.92
  247.6 5.4 %bitcast_add_fusion.5 = f32[32,16,1024]{2,1,0:T(8,128)} fusion(f32[32,16,1024]{2,1,0:T(8,128)} %get-tuple-element.390, f32[11,32,1024]{2,0,1:T(8,128)S(1)} %stack.92, pred[]{:T(512)S(6)} %compare.5, f32[16]{0:T(128)} %get-tuple-element.352, f32[16]{0:T(128)S(1)} %get-tuple-element.353, f32[11]{0:T(128)S(1)} %add_convert_fusion.2, ...), kind=kOutput, calls=%fused_computation.4.clone.1 | convolution fusion | flops 70255472 | bytes 5636397 | tf_op jit(solution)/shard_map/while/body/eval_jaxpr/is,scj->cij/dot_general | solution.py:73
  257.7 2.3 stack.92
  260.0 5.4 %bitcast_add_fusion.5 = f32[32,16,1024]{2,1,0:T(8,128)} fusion(f32[32,16,1024]{2,1,0:T(8,128)} %get-tuple-element.390, f32[11,32,1024]{2,0,1:T(8,128)S(1)} %stack.92, pred[]{:T(512)S(6)} %compare.5, f32[16]{0:T(128)} %get-tuple-element.352, f32[16]{0:T(128)S(1)} %get-tuple-element.353, f32[11]{0:T(128)S(1)} %add_convert_fusion.2, ...), kind=kOutput, calls=%fused_computation.4.clone.1 | convolution fusion | flops 70255472 | bytes 5636397 | tf_op jit(solution)/shard_map/while/body/eval_jaxpr/is,scj->cij/dot_general | solution.py:73
  265.4 6.3 %copy.96 = f32[32,16,1024]{0,2,1:T(8,128)} copy(f32[32,16,1024]{2,1,0:T(8,128)} %get-tuple-element.409) | data formatting | bytes 4194304 | tf_op jit(solution)/shard_map/while | solution.py:77
  271.7 4.3 fusion.34
  276.0 62.1 %maximum_convert_fusion.4 = bf16[32,16,16,1024]{0,1,3,2:T(8,128)(2,1)} fusion(bf16[32,1,16,1024]{0,3,2,1:T(8,128)(2,1)S(1)} %fusion.34, bf16[16,1,3,3]{0,3,2,1:T(4,128)(2,1)S(1)} %copy-done), kind=kOutput, calls=%fused_computation.44.clone.clone.1 | convolution fusion | flops 161386496 | bytes 17826080 | tf_op jit(solution)/shard_map/conv_general_dilated | solution.py:84
  338.1 82.2 %fusion.28 = f32[32,1,16,1024]{0,1,3,2:T(1,128)} fusion(bf16[1,16,3,3]{1,3,2,0:T(4,128)(2,1)S(1)} %copy-done.7, bf16[32,16,16,1024]{0,1,3,2:T(8,128)(2,1)} %maximum_convert_fusion.4), kind=kOutput, calls=%fused_computation.45 | convolution fusion | flops 144609280 | bytes 18874656 | tf_op jit(solution)/shard_map/conv_general_dilated | solution.py:88
  420.3 10.0 %add_bitcast_fusion = f32[1,32,16,1024]{1,3,2,0:T(8,128)} fusion(f32[32,16,1024]{0,2,1:T(8,128)} %bitcast.169, f32[32,16,1024]{0,2,1:T(8,128)} %copy.96), kind=kLoop, calls=%fused_computation.51 | loop fusion | flops 1048576 | bytes 6291456 | tf_op jit(solution)/shard_map/broadcast_in_dim | solution.py:166
  430.3 6.4 %copy.100 = f32[1,32,16,1024]{3,2,1,0:T(8,128)} copy(f32[1,32,16,1024]{1,3,2,0:T(8,128)} %add_bitcast_fusion) | data formatting | bytes 4194304 | tf_op jit(solution)/shard_map/broadcast_in_dim | solution.py:166
  (184 shorter events, 45.6 us)
Async XLA Ops:
  6.5 269.5 %copy-start = (bf16[16,1,3,3]{0,3,2,1:T(4,128)(2,1)S(1)}, bf16[16,1,3,3]{0,3,2,1:T(4,128)(2,1)}, u32[]{:S(2)}) copy-start(bf16[16,1,3,3]{0,3,2,1:T(4,128)(2,1)} %param.22) | copy-start | bytes 868
  11.7 33.0 %all-to-all-start = ((bf16[8,2,2,128,128]{4,3,2,1,0:T(8,128)(2,1)}), bf16[8,2,2,128,128]{4,3,2,1,0:T(8,128)(2,1)S(1)}, u32[]{:S(2)}, u32[]{:S(2)}) async-start(bf16[8,2,2,128,128]{4,3,2,1,0:T(8,128)(2,1)} %bitcast.64), calls=%async_computation | async-start | bytes 2097152 | tf_op jit(solution)/shard_map/all_to_all | solution.py:122
  47.0 1.0 copy-start.4
  50.6 4.7 %copy-start.5 = (f32[2,128,128]{2,1,0:T(8,128)S(1)}, f32[2,128,128]{2,1,0:T(8,128)}, u32[]{:S(2)}) copy-start(f32[2,128,128]{2,1,0:T(8,128)} %param.16) | copy-start | bytes 393220
  51.7 29.6 %all-to-all-start.1 = ((bf16[8,2,2,128,128]{4,3,2,1,0:T(8,128)(2,1)}), bf16[8,2,2,128,128]{4,3,2,1,0:T(8,128)(2,1)S(1)}, u32[]{:S(2)}, u32[]{:S(2)}) async-start(bf16[8,2,2,128,128]{4,3,2,1,0:T(8,128)(2,1)} %copy.92), calls=%async_computation.1 | async-start | bytes 2097152 | tf_op jit(solution)/shard_map/all_to_all | solution.py:126
  55.3 149.3 %reduce-scatter.2.cloned.1.call-start = ((), (), s32[]{:S(2)}) async-start(), calls=%async_computation.4 | async-start | bytes 1179648 | tf_op jit(solution)/shard_map/reduce_scatter | solution.py:144
  82.2 0.7 copy-start.8
  82.2 0.7 copy-start.9
  140.1 1.2 copy-start.6
  206.3 10.3 %copy-start.10 = (f32[4]{0:T(128)S(1)}, f32[4]{0:T(128)}, u32[]{:S(2)}) copy-start(f32[4]{0:T(128)} %param.21) | copy-start | bytes 52
  207.1 9.4 %all-to-all-start.2 = ((bf16[4,32,1024]{2,1,0:T(8,128)(2,1)}), bf16[4,32,1024]{2,1,0:T(8,128)(2,1)S(1)}, u32[]{:S(2)}, u32[]{:S(2)}) async-start(bf16[4,32,1024]{2,1,0:T(8,128)(2,1)} %multiply_convert_fusion.1), calls=%async_computation.3 | async-start | bytes 524288 | tf_op jit(solution)/shard_map/all_to_all | solution.py:157
  216.6 2.7 copy-start.2
  223.6 4.5 %copy-start.3 = (f32[4,32,1024]{2,1,0:T(8,128)S(1)}, f32[4,32,1024]{2,1,0:T(8,128)}, u32[]{:S(2)}) copy-start(f32[4,32,1024]{2,1,0:T(8,128)} %copy-done.2) | copy-start | bytes 1572868 | tf_op jit(solution)/shard_map/while
  223.6 4.5 %copy-start.11 = (f32[4]{0:T(128)S(1)}, f32[4]{0:T(128)}, u32[]{:S(2)}) copy-start(f32[4]{0:T(128)} %get-tuple-element.414) | copy-start | bytes 52 | tf_op jit(solution)/shard_map/while
  228.1 2.7 copy-start.2
  235.1 5.4 %copy-start.3 = (f32[4,32,1024]{2,1,0:T(8,128)S(1)}, f32[4,32,1024]{2,1,0:T(8,128)}, u32[]{:S(2)}) copy-start(f32[4,32,1024]{2,1,0:T(8,128)} %copy-done.2) | copy-start | bytes 1572868 | tf_op jit(solution)/shard_map/while
  235.1 5.4 %copy-start.11 = (f32[4]{0:T(128)S(1)}, f32[4]{0:T(128)}, u32[]{:S(2)}) copy-start(f32[4]{0:T(128)} %get-tuple-element.414) | copy-start | bytes 52 | tf_op jit(solution)/shard_map/while
  240.5 2.7 copy-start.2
  247.5 5.4 %copy-start.3 = (f32[4,32,1024]{2,1,0:T(8,128)S(1)}, f32[4,32,1024]{2,1,0:T(8,128)}, u32[]{:S(2)}) copy-start(f32[4,32,1024]{2,1,0:T(8,128)} %copy-done.2) | copy-start | bytes 1572868 | tf_op jit(solution)/shard_map/while
  247.6 5.4 %copy-start.11 = (f32[4]{0:T(128)S(1)}, f32[4]{0:T(128)}, u32[]{:S(2)}) copy-start(f32[4]{0:T(128)} %get-tuple-element.414) | copy-start | bytes 52 | tf_op jit(solution)/shard_map/while
  253.0 2.7 copy-start.2
  260.0 5.4 %copy-start.3 = (f32[4,32,1024]{2,1,0:T(8,128)S(1)}, f32[4,32,1024]{2,1,0:T(8,128)}, u32[]{:S(2)}) copy-start(f32[4,32,1024]{2,1,0:T(8,128)} %copy-done.2) | copy-start | bytes 1572868 | tf_op jit(solution)/shard_map/while
  260.0 5.4 %copy-start.11 = (f32[4]{0:T(128)S(1)}, f32[4]{0:T(128)}, u32[]{:S(2)}) copy-start(f32[4]{0:T(128)} %get-tuple-element.414) | copy-start | bytes 52 | tf_op jit(solution)/shard_map/while
  276.0 62.1 %copy-start.7 = (bf16[1,16,3,3]{1,3,2,0:T(4,128)(2,1)S(1)}, bf16[1,16,3,3]{1,3,2,0:T(4,128)(2,1)}, u32[]{:S(2)}) copy-start(bf16[1,16,3,3]{1,3,2,0:T(4,128)(2,1)} %param.23) | copy-start | bytes 868
  430.3 6.4 %copy-start.1 = (bf16[16,1,3,3]{0,3,2,1:T(4,128)(2,1)S(1)}, bf16[16,1,3,3]{0,3,2,1:T(4,128)(2,1)}, u32[]{:S(2)}) copy-start(bf16[16,1,3,3]{0,3,2,1:T(4,128)(2,1)} %param.22) | copy-start | bytes 868
Sparse Core Ops, SparseCore 0:
  141.4 63.1 reduce-scatter.1
where the time goes:
time: 445 us; the launch traced here: 444 us
  matrix products  168 us (38%)
  waiting for transfers between devices  120 us (27%)
  local copies, waits for them, and re-layouts  66.2 us (15%)
  loops' own time  31.9 us (7%)
  other arithmetic  29.9 us (7%)
  starting transfers between devices  14.5 us (3%)
  between operations  13.7 us (3%)
    conv_general_dilated x1, matrix products, prior(): lax.conv_general_dilated(hidden, prior_out.astype(jnp.float32), (1, 1), '...  82.2 us
    reduce_scatter x1, waiting for transfers between devices, body(): lax.psum_scatter(canvas.astype(jnp.bfloat16), 'tile', scatter_dimension=0...  62.9 us
    conv_general_dilated x1, matrix products, prior(): lax.conv_general_dilated(rounded, prior_in.astype(jnp.float32), (1, 1), '...  62.1 us
    another operation x1, loops' own time, body(): canvas = lax.fori_loop(0, count, place, jnp.zeros((H, width), jnp.float32))  31.3 us
    all_to_all x1, waiting for transfers between devices, body(): lax.all_to_all(fixed.reshape(tiles, depth, 2, side, side), 'tile', split_...  25.9 us
    all_to_all x1, waiting for transfers between devices, body(): lax.all_to_all(packed.reshape(tiles, depth, 2, side, side), 'tile', split...  25.2 us
    dot_general x4, matrix products, add_angle(): jnp.einsum('is,scj->cij', weights, columns_stack, precision=lax.Precision...  20.6 us
    dynamic_update_slice x8, local copies, waits for them, and re-layouts, place(): return lax.dynamic_update_slice(canvas, piece, (row, col))  15.7 us
  transfers between devices with their start and end apart: 4, of which 4 were waited for; matrix products, arithmetic and copies ran while one was open for 0% of the time, Pallas kernels for 0%

commit v1 on v0

v1 whole, which is shorter than its diff:
```python
import functools

import jax
import jax.numpy as jnp
import numpy as np
from jax import lax
from jax.experimental import pallas as pl
from jax.experimental.pallas import tpu as pltpu
from jax.sharding import PartitionSpec as P

H = 512
W = 1024
XW = 16
LANES = 128
SUBLANES = 8
PACK = 16
BEND = 3
REACH = BEND + 1
EDGE = BEND
TILE = 256
PAIR = 2
VMEM_LIMIT = 24 * 1024 * 1024


def dft_table(side):
    index = np.arange(side)
    phase = (index[:, None] * index[None, :] % side).astype(np.float64) * (2.0 * np.pi / side)
    scale = 1.0 / np.sqrt(side)
    real = np.cos(phase) * scale
    imag = -np.sin(phase) * scale
    table = np.block([[real, imag], [-imag, real]]).astype(np.float32)
    return jnp.asarray(table.astype(jnp.bfloat16))


def dot(left, right, precision=None):
    return jnp.dot(left, right, preferred_element_type=jnp.float32, precision=precision)


def swap_halves(values, pair, side):
    return jnp.concatenate(
        [
            jnp.concatenate(
                [values[k * side : (k + 1) * side, h * side : (h + 1) * side] for k in range(pair)], axis=1
            )
            for h in range(2)
        ],
        axis=0,
    )


def ahead(axis, step, size):
    return lax.rem(lax.axis_index(axis) + step, size)


def behind(axis, step, size):
    return lax.rem(lax.axis_index(axis) + (size - step), size)


def rotate(values, axis, size):
    ring = len(values)
    return [values[0]] + [
        lax.ppermute(values[step], axis, [(a, a // ring * ring + (a + step) % ring) for a in range(size)])
        for step in range(1, ring)
    ]


def deal_kernel(tiles, frames_ref, *refs):
    sources, out_refs, targets, sems = refs[:3], refs[3 : 3 + tiles], refs[3 + tiles : 6 + tiles], refs[-1]
    depth = out_refs[0].shape[0]
    copies = [
        pltpu.make_async_copy(
            frames_ref.at[pl.ds(ahead("tile", step, tiles) * depth, depth)], out_refs[step], sems.at[step]
        )
        for step in range(tiles)
    ]
    copies += [
        pltpu.make_async_copy(source, target, sems.at[tiles + k])
        for k, (source, target) in enumerate(zip(sources, targets))
    ]
    for copy in copies:
        copy.start()
    for copy in copies:
        copy.wait()


def deal(frames, tiles, *others):
    depth = frames.shape[0] // tiles
    results = pl.pallas_call(
        functools.partial(deal_kernel, tiles),
        out_shape=(pltpu.VMEM((depth,) + frames.shape[1:], frames.dtype),) * tiles
        + tuple(pltpu.VMEM(x.shape, x.dtype) for x in others),
        in_specs=[pl.BlockSpec(memory_space=pltpu.HBM)] * (1 + len(others)),
        out_specs=(pl.BlockSpec(memory_space=pltpu.VMEM),) * (tiles + len(others)),
        scratch_shapes=[pltpu.SemaphoreType.DMA((tiles + len(others),))],
        compiler_params=pltpu.CompilerParams(vmem_limit_bytes=VMEM_LIMIT),
        name="deal",
    )(*[pltpu.with_memory_space_constraint(x, pltpu.HBM) for x in (frames, *others)])
    return list(results[:tiles]), *results[tiles:]


def turned_table(table):
    side = table.shape[0] // 2
    return jnp.concatenate(
        [
            jnp.concatenate([table[:side, :side], table[side:, :side]], axis=1),
            jnp.concatenate([table[:side, side:], table[side:, side:]], axis=1),
        ],
        axis=0,
    )


def prepare_kernel(patch_ref, table_ref, unit_ref):
    count, _, side, _ = patch_ref.shape
    table = table_ref[...]
    left = turned_table(table)
    for first in range(0, count, PAIR):
        joined = jnp.concatenate(
            [jnp.concatenate([patch_ref[k, 0], patch_ref[k, 1]], axis=1) for k in range(first, first + PAIR)],
            axis=0,
        )
        half = dot(joined, table).astype(jnp.bfloat16)
        spectrum = dot(left, swap_halves(half, PAIR, side))
        real = spectrum[:side]
        imag = spectrum[side:]
        factor = lax.rsqrt(real * real + imag * imag + 0.25)
        cut = slice(first * side, (first + PAIR) * side)
        unit_ref[:side, cut] = real * factor
        unit_ref[side:, cut] = imag * factor


def prepare(waves, table):
    count, _, side, _ = waves.shape
    vmem = pl.BlockSpec(memory_space=pltpu.VMEM)
    return pl.pallas_call(
        prepare_kernel,
        out_shape=pltpu.VMEM((2 * side, count * side), jnp.float32),
        in_specs=[vmem] * 2,
        out_specs=vmem,
        compiler_params=pltpu.CompilerParams(vmem_limit_bytes=VMEM_LIMIT),
        name="prepare",
    )(waves, table)


def project_kernel(tiles, place_ref, unit_ref, probe_ref, table_ref, *refs):
    level_refs, out_refs = refs[:tiles], refs[tiles : 2 * tiles]
    canvas, levels = refs[2 * tiles :]
    depth, side = level_refs[0].shape[:2]
    count = unit_ref.shape[1] // side
    for step, level_ref in enumerate(level_refs):
        levels[step * depth : (step + 1) * depth] = level_ref[...]
    owner = [place_ref[0, k] for k in range(count)]
    slots = []
    for k in range(count):
        rank = jnp.int32(0)
        for j in range(k):
            rank = rank + jnp.where(owner[j] == owner[k], 1, 0)
        slots.append(behind("tile", owner[k], tiles) * depth + rank)
    table = table_ref[...]
    left = turned_table(table)
    canvas[...] = jnp.zeros_like(canvas)
    tall = side + SUBLANES
    lane = lax.broadcasted_iota(jnp.int32, (tall, side), 1)
    for first in range(0, count, PAIR):
        level = [levels[slots[k]].astype(jnp.float32) for k in range(first, first + PAIR)]
        level = jnp.concatenate(level, axis=1)
        cut = slice(first * side, (first + PAIR) * side)
        real = (unit_ref[:side, cut] * level).astype(jnp.bfloat16)
        imag = (unit_ref[side:, cut] * level).astype(jnp.bfloat16)
        target = jnp.concatenate(
            [
                jnp.concatenate([real[:, k * side : (k + 1) * side], imag[:, k * side : (k + 1) * side]], axis=1)
                for k in range(PAIR)
            ],
            axis=0,
        )
        back = dot(target, left).astype(jnp.bfloat16)
        result = dot(table, swap_halves(back, PAIR, side))
        for k in range(PAIR):
            fixed_re = result[:side, k * side : (k + 1) * side]
            fixed_im = result[side:, k * side : (k + 1) * side]
            contrib = probe_ref[0] * fixed_im - probe_ref[1] * fixed_re
            row = place_ref[1, first + k]
            col = place_ref[2, first + k]
            down = lax.rem(row, SUBLANES)
            shift = lax.rem(col, LANES)
            top = pl.multiple_of(row - down, SUBLANES)
            base = pl.multiple_of(col - shift, LANES)
            turned = jnp.concatenate([contrib, jnp.zeros((SUBLANES, side), jnp.float32)], axis=0)
            turned = pltpu.roll(pltpu.roll(turned, down, 0), shift, 1)
            piece = jnp.concatenate(
                [jnp.where(lane >= shift, turned, 0.0), jnp.where(lane < shift, turned, 0.0)], axis=1
            )
            where = (pl.ds(top, tall), pl.ds(base, 2 * side))
            canvas[where] = canvas[where] + piece
    strip_rows, width = out_refs[0].shape
    half = tiles // 2
    me = lax.axis_index("tile")
    place = lax.rem(me, half)
    for step in range(half):
        turn = lax.rem(place + step, half)
        near = pl.multiple_of((me - place + turn) * strip_rows, strip_rows)
        far = pl.multiple_of((half - (me - place) + turn) * strip_rows, strip_rows)
        out_refs[step][...] = canvas[pl.ds(near, strip_rows), :width].astype(jnp.bfloat16)
        out_refs[half + step][...] = canvas[pl.ds(far, strip_rows), :width].astype(jnp.bfloat16)


def project(place, unit, probe, table, levels):
    tiles = len(levels)
    depth, side = levels[0].shape[:2]
    smem = pl.BlockSpec(memory_space=pltpu.SMEM)
    vmem = pl.BlockSpec(memory_space=pltpu.VMEM)
    return pl.pallas_call(
        functools.partial(project_kernel, tiles),
        out_shape=(jax.ShapeDtypeStruct((H // tiles, W), jnp.bfloat16),) * tiles,
        in_specs=[smem] + [vmem] * (3 + tiles),
        out_specs=(vmem,) * tiles,
        scratch_shapes=[
            pltpu.VMEM((H + SUBLANES, W + side), jnp.float32),
            pltpu.VMEM((tiles * depth, side, side), levels[0].dtype),
        ],
        compiler_params=pltpu.CompilerParams(vmem_limit_bytes=VMEM_LIMIT),
        name="project",
    )(place, unit, probe, table, *levels)


def slabs_kernel(count, select_ref, *refs):
    strips = jnp.concatenate([ref[...] for ref in refs[:count]], axis=0)
    result = dot(select_ref[...], strips).astype(jnp.bfloat16)
    rowcap = refs[count].shape[0]
    for step, out_ref in enumerate(refs[count:]):
        out_ref[...] = result[step * rowcap : (step + 1) * rowcap]


def cut_slabs(select, strips, angles):
    rowcap = select.shape[0] // angles
    vmem = pl.BlockSpec(memory_space=pltpu.VMEM)
    return pl.pallas_call(
        functools.partial(slabs_kernel, len(strips)),
        out_shape=(jax.ShapeDtypeStruct((rowcap, strips[0].shape[1]), jnp.bfloat16),) * angles,
        in_specs=[vmem] * (1 + len(strips)),
        out_specs=(vmem,) * angles,
        compiler_params=pltpu.CompilerParams(vmem_limit_bytes=VMEM_LIMIT),
        name="cut_slabs",
    )(select, *strips)


def selection(length_ref, shape, strip_rows):
    angles = length_ref.shape[0]
    rowcap = shape[0] // angles
    row = lax.broadcasted_iota(jnp.int32, shape, 0)
    source = lax.broadcasted_iota(jnp.int32, shape, 1) % strip_rows
    wanted = jnp.full(shape, -1, jnp.int32)
    for step in range(angles):
        slab = ahead("angle", step, angles)
        start = jnp.int32(0)
        for q in range(angles):
            start = start + jnp.where(q < slab, length_ref[q], 0)
        within = row - step * rowcap
        good = (within >= 0) & (within < rowcap) & (within < length_ref[slab])
        wanted = jnp.where(good, within + start, wanted)
    return jnp.where(source == wanted, 1.0, 0.0).astype(jnp.bfloat16)


def weights_kernel(strip_rows, tan_ref, length_ref, first_ref, second_ref, out_ref, last_ref, select_ref, order_ref):
    angles = tan_ref.shape[0]
    channels = first_ref.shape[0]
    group = PACK // angles
    wide = channels * XW
    steps = 2 * REACH + 1
    exact = lax.Precision.HIGHEST

    shape = (3 * XW, TILE)
    line = lax.broadcasted_iota(jnp.int32, shape, 0)
    column = lax.broadcasted_iota(jnp.int32, shape, 1)
    dj = line // XW - 1
    offset = (line % XW).astype(jnp.float32) - (XW - 1) / 2.0
    step = column // PACK
    tangent = jnp.zeros(shape, jnp.float32)
    for a in range(angles):
        source = behind("angle", a, angles)
        tangent = jnp.where(column % angles == a, tan_ref[source], tangent)
    shifted = jnp.clip(offset * tangent, -float(BEND), float(BEND))
    floor_shift = jnp.floor(shifted)
    fraction = shifted - floor_shift

    def share(at):
        at = at.astype(jnp.float32)
        low = jnp.where(at == floor_shift, 1.0 - fraction, 0.0)
        return (low + jnp.where(at == floor_shift + 1.0, fraction, 0.0)) * (0.25 / angles)

    position = step - steps
    shear = jnp.where(step < steps, share(step - REACH - dj), 0.0)
    on_left = (position >= 0) & (position < EDGE) & (dj == -1)
    on_right = (position >= EDGE) & (position < 2 * EDGE) & (dj == 1)
    shear = shear - jnp.where(on_left, share(position + 1), 0.0) - jnp.where(on_right, share(EDGE - 1 - position), 0.0)

    tall = (wide, 3 * XW)
    line = lax.broadcasted_iota(jnp.int32, tall, 0)
    column = lax.broadcasted_iota(jnp.int32, tall, 1)
    spread = lax.broadcasted_iota(jnp.int32, (wide, channels), 0) // XW
    spread = (spread == lax.broadcasted_iota(jnp.int32, (wide, channels), 1)).astype(jnp.float32)
    taps = dot(spread, first_ref[...].astype(jnp.float32), exact)
    band = jnp.zeros(tall, jnp.float32)
    for di in range(3):
        for at in range(3):
            hit = (column % XW - line % XW == di - 1) & (column // XW == at)
            band = band + jnp.where(hit, taps[:, 3 * di + at : 3 * di + at + 1], 0.0)

    slab_row = lax.broadcasted_iota(jnp.int32, (wide, TILE), 1) % PACK // angles
    flat_row = lax.broadcasted_iota(jnp.int32, (XW, TILE), 1) % PACK // angles
    mixed = dot(band, shear, exact)
    for r in range(group):
        out_ref[r * wide : (r + 1) * wide, :] = jnp.where(slab_row == r, mixed, 0.0).astype(jnp.bfloat16)
        out_ref[group * wide + r * XW : group * wide + (r + 1) * XW, :] = jnp.where(
            flat_row == r, shear[XW : 2 * XW], 0.0
        ).astype(jnp.bfloat16)

    gather = lax.broadcasted_iota(jnp.int32, (channels, wide), 1) // XW
    gather = (gather == lax.broadcasted_iota(jnp.int32, (channels, wide), 0)).astype(jnp.float32)
    taps = dot(second_ref[...].astype(jnp.float32), gather, exact)
    line = lax.broadcasted_iota(jnp.int32, (XW, wide), 0)
    column = lax.broadcasted_iota(jnp.int32, (XW, wide), 1) % XW
    for at in range(3):
        total = jnp.zeros((XW, wide), jnp.float32)
        for di in range(3):
            total = total + jnp.where(column - line == di - 1, taps[3 * di + at : 3 * di + at + 1, :], 0.0)
        last_ref[at * XW : (at + 1) * XW, :] = total.astype(jnp.bfloat16)


    select_ref[...] = selection(length_ref, select_ref.shape, strip_rows)
    rows = order_ref.shape[0]
    line = lax.broadcasted_iota(jnp.int32, (rows, rows), 0)
    source = lax.broadcasted_iota(jnp.int32, (rows, rows), 1)
    hit = source == line % angles * (rows // angles) + line // angles
    order_ref[...] = jnp.where(hit, 1.0, 0.0).astype(jnp.bfloat16)


def make_weights(angle_tan, lengths, prior_in, prior_out, strip_rows, parts):
    angles = angle_tan.shape[0]
    channels = prior_in.shape[0]
    rows = PACK // angles * XW * (channels + 1)
    smem = pl.BlockSpec(memory_space=pltpu.SMEM)
    vmem = pl.BlockSpec(memory_space=pltpu.VMEM)
    return pl.pallas_call(
        functools.partial(weights_kernel, strip_rows),
        out_shape=(
            pltpu.VMEM((rows, TILE), jnp.bfloat16),
            pltpu.VMEM((3 * XW, channels * XW), jnp.bfloat16),
            pltpu.VMEM((2 * strip_rows, parts * strip_rows), jnp.bfloat16),
            pltpu.VMEM((2 * strip_rows, 2 * strip_rows), jnp.bfloat16),
        ),
        in_specs=[smem, smem, vmem, vmem],
        out_specs=(vmem,) * 4,
        compiler_params=pltpu.CompilerParams(vmem_limit_bytes=VMEM_LIMIT),
        name="make_weights",
    )(angle_tan, lengths, prior_in.reshape(channels, 9), prior_out.reshape(channels, 9).T)


def slide(values, by, lane):
    if by == 0:
        return values
    width = values.shape[1]
    turned = pltpu.roll(values, (-by) % width, 1)
    return jnp.where((lane < width - by) if by > 0 else (lane >= -by), turned, 0.0)


def volume_kernel(*refs):
    *piece_refs, first_ref, last_ref, order_ref, out_ref, ordered, even, odd, held, sems = refs
    angles = len(piece_refs)
    rowcap, width = piece_refs[0].shape
    rows = angles * rowcap
    group = PACK // angles
    groups = rowcap // group
    wide = last_ref.shape[1]
    tiles = width // TILE
    span = 2 * REACH + 1

    ordered[...] = dot(order_ref[...], jnp.concatenate([ref[...] for ref in piece_refs], axis=0))

    lane = lax.broadcasted_iota(jnp.int32, (PACK, width), 1)
    inside = lax.broadcasted_iota(jnp.int32, (PACK, LANES), 1)

    def stack_rows(here, target):
        taken = ordered[pl.ds(pl.multiple_of(here * PACK, PACK), PACK), :]
        moved = {by: slide(taken, by, lane) for by in range(-REACH, REACH + 1)}
        for by, value in moved.items():
            at = (by + REACH) * PACK
            target[at : at + PACK, :] = value.astype(jnp.bfloat16)
        for q in range(EDGE):
            at = (span + q) * PACK
            target[at : at + PACK, :LANES] = jnp.where(inside == 0, moved[q][:, :LANES], 0.0).astype(jnp.bfloat16)
            at += EDGE * PACK
            target[at : at + PACK, width - LANES :] = jnp.where(
                inside == LANES - 1, moved[-q][:, width - LANES :], 0.0
            ).astype(jnp.bfloat16)

    def copy_out(here):
        part = pl.ds(here * group, group)
        return pltpu.make_async_copy(held.at[part], out_ref.at[part], sems.at[here])

    def one_group(here, stack):
        base = []
        partial = [[] for _ in range(group)]
        waiting = None
        for n in range(tiles + 1):
            hidden = None
            if n < tiles:
                mixed = dot(first_ref[...], stack[:, n * TILE : (n + 1) * TILE])
                base.append(mixed[group * wide :])
                hidden = jnp.maximum(mixed[: group * wide].astype(jnp.bfloat16), 0.0)
            if waiting is not None:
                for r in range(group):
                    partial[r].append(dot(last_ref[...], waiting[r * wide : (r + 1) * wide]))
            waiting = hidden
        base = jnp.concatenate(base, axis=1)
        for r in range(group):
            sums = jnp.concatenate(partial[r], axis=1)
            held[here * group + r] = (
                base[r * XW : (r + 1) * XW]
                + sums[XW : 2 * XW]
                + slide(sums[:XW], -1, lane)
                + slide(sums[2 * XW :], 1, lane)
            )
        copy_out(here).start()

    even[span * PACK :, :] = jnp.zeros((TILE - span * PACK, width), jnp.bfloat16)
    odd[span * PACK :, :] = jnp.zeros((TILE - span * PACK, width), jnp.bfloat16)
    stack_rows(0, even)

    def two_groups(step, carry):
        here = 2 * step
        stack_rows(here + 1, odd)
        one_group(here, even)
        stack_rows(lax.rem(here + 2, groups), even)
        one_group(here + 1, odd)
        return carry

    lax.fori_loop(0, groups // 2, two_groups, 0)

    def finish(here, carry):
        copy_out(here).wait()
        return carry

    lax.fori_loop(0, groups, finish, 0)


def make_volume(pieces, first, last, order):
    angles = len(pieces)
    rowcap, width = pieces[0].shape
    vmem = pl.BlockSpec(memory_space=pltpu.VMEM)
    shape = (rowcap, XW, width)
    return pl.pallas_call(
        volume_kernel,
        out_shape=jax.ShapeDtypeStruct(shape, jnp.float32),
        in_specs=[vmem] * (angles + 3),
        out_specs=pl.BlockSpec(memory_space=pl.ANY),
        scratch_shapes=[
            pltpu.VMEM((angles * rowcap, width), jnp.float32),
            pltpu.VMEM((TILE, width), jnp.bfloat16),
            pltpu.VMEM((TILE, width), jnp.bfloat16),
            pltpu.VMEM(shape, jnp.float32),
            pltpu.SemaphoreType.DMA((rowcap * angles // PACK,)),
        ],
        compiler_params=pltpu.CompilerParams(vmem_limit_bytes=VMEM_LIMIT),
        name="make_volume",
    )(*pieces, first, last, order)


def body(
    patches,
    magnitudes,
    probe,
    owners,
    scan_rows,
    scan_cols,
    slab_rows,
    angle_tan,
    prior_in,
    prior_out,
):
    tiles = lax.axis_size("tile")
    angles = lax.axis_size("angle")
    half = tiles // 2
    levels, waves, probe, table = deal(magnitudes[0], tiles, patches[0], probe, dft_table(patches.shape[3]))
    levels = rotate(levels, "tile", tiles)
    place = jnp.stack([owners[0, :, 0], scan_rows[0], scan_cols[0]])
    waves, levels[1], levels[-1] = lax.optimization_barrier((waves, levels[1], levels[-1]))
    strips = project(place, prepare(waves, table), probe, table, levels)
    near, far = strips[:half], strips[half:]
    angle_tan, prior_in, prior_out, unused = lax.optimization_barrier(
        (angle_tan, prior_in, prior_out, near[0])
    )
    first, last, select, order = make_weights(
        angle_tan, slab_rows[0], prior_in, prior_out, H // tiles, half + 1
    )
    far = rotate(far, "tile", tiles)
    far = sum(part.astype(jnp.float32) for part in far).astype(jnp.bfloat16)
    far, *near = lax.optimization_barrier((far, *near))
    far = lax.ppermute(far, "tile", [(a, (a + half) % tiles) for a in range(tiles)])
    near = rotate(near, "tile", tiles)
    select, near[0] = lax.optimization_barrier((select, near[0]))
    slabs = cut_slabs(select, [far] + near, angles)
    return make_volume(rotate(slabs, "angle", angles), first, last, order)[None]


def solution(mesh):
    placed = (
        P("angle", "tile", None, None, None),
        P("angle", "tile", None, None),
        P(),
        P("angle", "tile", None),
        P("angle", "tile"),
        P("angle", "tile"),
        P("tile", None),
        P(),
        P(),
        P(),
    )
    return jax.shard_map(
        body, mesh=mesh, in_specs=placed, out_specs=P("tile", "angle", None, None), check_vma=False
    )
```

time: 445 us -> 55.7 us (0.13)
  matrix products: 168 us -> 0 us
  waiting for transfers between devices: 120 us -> 11.5 us
  local copies, waits for them, and re-layouts: 66.2 us -> 0.15 us
  loops' own time: 31.9 us -> 0 us
  other arithmetic: 29.9 us -> 0.77 us
  Pallas kernels: 0 us -> 15.1 us
  between operations: 13.7 us -> 0.12 us
  starting transfers between devices: 14.5 us -> 27.5 us
    conv_general_dilated x2 -> x0, matrix products: 144 us -> none  [the longest x1 82.2 us: prior(): lax.conv_general_dilated(hidden, prior_out.astype(jnp.float32), (1, 1), '...]
    reduce_scatter x1 -> x0, waiting for transfers between devices: 62.9 us -> none  [body(): lax.psum_scatter(canvas.astype(jnp.bfloat16), 'tile', scatter_dimension=0...]
    all_to_all x3 -> x0, waiting for transfers between devices: 56.9 us -> none  [the longest x1 25.9 us: body(): lax.all_to_all(fixed.reshape(tiles, depth, 2, side, side), 'tile', split_...]
    another operation x2 -> x0, loops' own time: 31.9 us -> none  [the longest x1 31.3 us: body(): canvas = lax.fori_loop(0, count, place, jnp.zeros((H, width), jnp.float32))]
    ppermute x0 -> x17, starting transfers between devices: none -> 27.5 us  [the longest x16 25.5 us: rotate(): lax.ppermute(values[step], axis, [(a, a // ring * ring + (a + step) % rin...]
    dot_general x10 -> x0, matrix products: 23.3 us -> none  [the longest x4 20.6 us: add_angle(): jnp.einsum('is,scj->cij', weights, columns_stack, precision=lax.Precision...]
    another operation x45 -> x0, local copies, waits for them, and re-layouts: 15.7 us -> none  [the longest x44 14.5 us: add_angle(): jnp.stack([padded[:, step:step + width] for step in range(2 * spread_cols...]
    dynamic_update_slice x8 -> x0, local copies, waits for them, and re-layouts: 15.7 us -> none  [place(): return lax.dynamic_update_slice(canvas, piece, (row, col))]
  transfers between devices with their start and end apart: 4 -> 17, of which waited for: 4 -> 11; matrix products, arithmetic and copies ran while one was open for 0% -> 1% of each run, Pallas kernels for 0% -> 5%
where the time goes in v1:
time: 55.7 us; the launch traced here: 55.2 us
  starting transfers between devices  27.5 us (49%)
  Pallas kernels  15.1 us (27%)
  waiting for transfers between devices  11.5 us (21%)
  other arithmetic  0.77 us (1%)
    ppermute x16, starting transfers between devices, rotate(): lax.ppermute(values[step], axis, [(a, a // ring * ring + (a + step) % rin...  25.5 us
    ppermute x16, waiting for transfers between devices, rotate(): lax.ppermute(values[step], axis, [(a, a // ring * ring + (a + step) % rin...  11 us
    pallas_call x1, Pallas kernels, make_volume(): pl.pallas_call(volume_kernel, out_shape=jax.ShapeDtypeStruct(shape, jnp.f...  9.35 us
    ppermute x1, starting transfers between devices, body(): lax.ppermute(far, 'tile', [(a, (a + half) % tiles) for a in range(tiles)])  1.97 us
    pallas_call x1, Pallas kernels, make_weights(): pl.pallas_call(functools.partial(weights_kernel, strip_rows), out_shape=(...  1.86 us
    pallas_call x1, Pallas kernels, project(): pl.pallas_call(functools.partial(project_kernel, tiles), out_shape=(jax.S...  1.53 us
    pallas_call x1, Pallas kernels, deal(): pl.pallas_call(functools.partial(deal_kernel, tiles), out_shape=(pltpu.VM...  1.46 us
  transfers between devices with their start and end apart: 17, of which 11 were waited for; matrix products, arithmetic and copies ran while one was open for 1% of the time, Pallas kernels for 5%

profile of v1, /device:TPU:0, one launch (start us, length us, event | category | flops | bytes accessed | tf_op | source)
XLA Modules:
  0.0 55.2 jit_solution(7098020365871309813)
XLA Ops:
  0.0 1.5 %deal.1 = (bf16[2,128,128]{2,1,0:T(8,128)(2,1)S(1)}, bf16[2,128,128]{2,1,0:T(8,128)(2,1)S(1)}, bf16[2,128,128]{2,1,0:T(8,128)(2,1)S(1)}, bf16[2,128,128]{2,1,0:T...) custom-call(bf16[16,128,128]{2,1,0:T(8,128)(2,1)} %bitcast.12, ...), custom_call_target="tpu_custom_call" | custom-call | tf_op jit(solution)/shard_map/deal/pallas_call | solution.py:88
  1.5 3.0 %collective-permute-start = (bf16[2,128,128]{2,1,0:T(8,128)(2,1)S(1)}, bf16[2,128,128]{2,1,0:T(8,128)(2,1)S(1)}, u32[]{:S(2)}, u32[]{:S(2)}) collective-permute-start(bf16[2,128,128]{2,1,0:T(8,128)(2,1)S(1)} %get-tuple-element.46), channel_id=1, source_target_pairs={{0,1},{1,2},{2,3},{3,4},{4,5},{5,6},{6,7},{7,0},{8,9},{9,10},{10,1... | collective-permute-start | bytes 196616 | tf_op jit(solution)/shard_map/ppermute | solution.py:62
  4.5 3.1 %collective-permute-start.1 = (bf16[2,128,128]{2,1,0:T(8,128)(2,1)S(1)}, bf16[2,128,128]{2,1,0:T(8,128)(2,1)S(1)}, u32[]{:S(2)}, u32[]{:S(2)}) collective-permute-start(bf16[2,128,128]{2,1,0:T(8,128)(2,1)S(1)} %get-tuple-element.47), channel_id=1, source_target_pairs={{0,7},{1,0},{2,1},{3,2},{4,3},{5,4},{6,5},{7,6},{8,15},{9,8},{10,9... | collective-permute-start | bytes 196616 | tf_op jit(solution)/shard_map/ppermute | solution.py:62
  7.6 1.5 %collective-permute-start.3 = (bf16[2,128,128]{2,1,0:T(8,128)(2,1)S(1)}, bf16[2,128,128]{2,1,0:T(8,128)(2,1)S(1)}, u32[]{:S(2)}, u32[]{:S(2)}) collective-permute-start(bf16[2,128,128]{2,1,0:T(8,128)(2,1)S(1)} %get-tuple-element.54), channel_id=1, source_target_pairs={{0,3},{1,4},{2,5},{3,6},{4,7},{5,0},{6,1},{7,2},{8,11},{9,12},{10,... | collective-permute-start | bytes 196616 | tf_op jit(solution)/shard_map/ppermute | solution.py:62
  9.1 1.2 %collective-permute-start.4 = (bf16[2,128,128]{2,1,0:T(8,128)(2,1)S(1)}, bf16[2,128,128]{2,1,0:T(8,128)(2,1)S(1)}, u32[]{:S(2)}, u32[]{:S(2)}) collective-permute-start(bf16[2,128,128]{2,1,0:T(8,128)(2,1)S(1)} %get-tuple-element.55), channel_id=1, source_target_pairs={{0,4},{1,5},{2,6},{3,7},{4,0},{5,1},{6,2},{7,3},{8,12},{9,13},{10,... | collective-permute-start | bytes 196616 | tf_op jit(solution)/shard_map/ppermute | solution.py:62
  10.3 3.6 %collective-permute-start.5 = (bf16[2,128,128]{2,1,0:T(8,128)(2,1)S(1)}, bf16[2,128,128]{2,1,0:T(8,128)(2,1)S(1)}, u32[]{:S(2)}, u32[]{:S(2)}) collective-permute-start(bf16[2,128,128]{2,1,0:T(8,128)(2,1)S(1)} %get-tuple-element.56), channel_id=1, source_target_pairs={{0,5},{1,6},{2,7},{3,0},{4,1},{5,2},{6,3},{7,4},{8,13},{9,14},{10,... | collective-permute-start | bytes 196616 | tf_op jit(solution)/shard_map/ppermute | solution.py:62
  13.9 1.3 %collective-permute-start.6 = (bf16[2,128,128]{2,1,0:T(8,128)(2,1)S(1)}, bf16[2,128,128]{2,1,0:T(8,128)(2,1)S(1)}, u32[]{:S(2)}, u32[]{:S(2)}) collective-permute-start(bf16[2,128,128]{2,1,0:T(8,128)(2,1)S(1)} %get-tuple-element.57), channel_id=1, source_target_pairs={{0,6},{1,7},{2,0},{3,1},{4,2},{5,3},{6,4},{7,5},{8,14},{9,15},{10,... | collective-permute-start | bytes 196616 | tf_op jit(solution)/shard_map/ppermute | solution.py:62
  15.2 0.7 %pad_add_fusion.place_ref = s32[3,8]{1,0:T(4,128)S(1)} fusion(s32[1,8]{1,0:T(1,128)} %param.16, s32[1,8]{1,0:T(1,128)} %param.15, s32[1,8]{1,0:T(1,128)} %bitcast.14), kind=kLoop, calls=%fused_computation.1 | loop fusion | flops 48 | bytes 192 | tf_op jit(solution)/shard_map/stack | solution.py:486
  16.0 0.6 %prepare.1.unit_ref = f32[256,1024]{1,0:T(8,128)S(1)} custom-call(bf16[8,2,128,128]{3,2,1,0:T(8,128)(2,1)S(1)} %get-tuple-element.48.patch_ref, bf16[256,256]{1,0:T(8,128)(2,1)S(1)} %get-tuple-element.49.table_ref), custom_call_target="tpu_custom_call" | custom-call | tf_op jit(solution)/shard_map/prepare/pallas_call | solution.py:134
  16.6 2.3 %collective-permute-done.4.refs_4_ = bf16[2,128,128]{2,1,0:T(8,128)(2,1)S(1)} collective-permute-done((bf16[2,128,128]{2,1,0:T(8,128)(2,1)S(1)}, bf16[2,128,128]{2,1,0:T(8,128)(2,1)S(1)}, u32[]{:S(2)}, u32[]{:S(2)}) %collective-permute-start.4) | collective-permute-done | bytes 65568 | tf_op jit(solution)/shard_map/ppermute | solution.py:62
  18.9 0.6 %collective-permute-done.6.refs_6_ = bf16[2,128,128]{2,1,0:T(8,128)(2,1)S(1)} collective-permute-done((bf16[2,128,128]{2,1,0:T(8,128)(2,1)S(1)}, bf16[2,128,128]{2,1,0:T(8,128)(2,1)S(1)}, u32[]{:S(2)}, u32[]{:S(2)}) %collective-permute-start.6) | collective-permute-done | bytes 65568 | tf_op jit(solution)/shard_map/ppermute | solution.py:62
  19.6 1.5 %project.1 = (bf16[64,1024]{1,0:T(8,128)(2,1)S(1)}, bf16[64,1024]{1,0:T(8,128)(2,1)S(1)}, bf16[64,1024]{1,0:T(8,128)(2,1)S(1)}, bf16[64,1024]{1,0:T(8,128)(2,1)S...) custom-call(s32[3,8]{1,0:T(4,128)S(1)} %pad_add_fusion.place_ref, ...), custom_call_target="tpu_custom_call" | custom-call | tf_op jit(solution)/shard_map/project/pallas_call | solution.py:212
  21.1 2.2 %collective-permute-start.7 = (bf16[64,1024]{1,0:T(8,128)(2,1)S(1)}, bf16[64,1024]{1,0:T(8,128)(2,1)S(1)}, u32[]{:S(2)}, u32[]{:S(2)}) collective-permute-start(bf16[64,1024]{1,0:T(8,128)(2,1)S(1)} %get-tuple-element.65), channel_id=1, source_target_pairs={{0,1},{1,2},{2,3},{3,0},{4,5},{5,6},{6,7},{7,4},{8,9},{9,10},{10,1... | collective-permute-start | bytes 393224 | tf_op jit(solution)/shard_map/ppermute | solution.py:62
  23.4 2.8 %collective-permute-start.9 = (bf16[64,1024]{1,0:T(8,128)(2,1)S(1)}, bf16[64,1024]{1,0:T(8,128)(2,1)S(1)}, u32[]{:S(2)}, u32[]{:S(2)}) collective-permute-start(bf16[64,1024]{1,0:T(8,128)(2,1)S(1)} %get-tuple-element.67), channel_id=1, source_target_pairs={{0,3},{1,0},{2,1},{3,2},{4,7},{5,4},{6,5},{7,6},{8,11},{9,8},{10,9... | collective-permute-start | bytes 393224 | tf_op jit(solution)/shard_map/ppermute | solution.py:62
  26.2 1.7 %collective-permute-done.7 = bf16[64,1024]{1,0:T(8,128)(2,1)S(1)} collective-permute-done((bf16[64,1024]{1,0:T(8,128)(2,1)S(1)}, bf16[64,1024]{1,0:T(8,128)(2,1)S(1)}, u32[]{:S(2)}, u32[]{:S(2)}) %collective-permute-start.7) | collective-permute-done | bytes 131104 | tf_op jit(solution)/shard_map/ppermute | solution.py:62
  28.0 1.0 %collective-permute-done.8 = bf16[64,1024]{1,0:T(8,128)(2,1)S(1)} collective-permute-done((bf16[64,1024]{1,0:T(8,128)(2,1)S(1)}, bf16[64,1024]{1,0:T(8,128)(2,1)S(1)}, u32[]{:S(2)}, u32[]{:S(2)}) %collective-permute-start.8) | collective-permute-done | bytes 131104 | tf_op jit(solution)/shard_map/ppermute | solution.py:62
  28.9 0.6 %collective-permute-done.9 = bf16[64,1024]{1,0:T(8,128)(2,1)S(1)} collective-permute-done((bf16[64,1024]{1,0:T(8,128)(2,1)S(1)}, bf16[64,1024]{1,0:T(8,128)(2,1)S(1)}, u32[]{:S(2)}, u32[]{:S(2)}) %collective-permute-start.9) | collective-permute-done | bytes 131104 | tf_op jit(solution)/shard_map/ppermute | solution.py:62
  29.6 2.0 %collective-permute-start.10 = (bf16[64,1024]{1,0:T(8,128)(2,1)S(1)}, bf16[64,1024]{1,0:T(8,128)(2,1)S(1)}, u32[]{:S(2)}, u32[]{:S(2)}) collective-permute-start(bf16[64,1024]{1,0:T(8,128)(2,1)S(1)} %add_convert_fusion), channel_id=1, source_target_pairs={{0,4},{1,5},{2,6},{3,7},{4,0},{5,1},{6,2},{7,3},{8,12},{9,13},{10,... | collective-permute-start | bytes 393224 | tf_op jit(solution)/shard_map/ppermute | solution.py:499
  31.6 1.5 %collective-permute-start.11 = (bf16[64,1024]{1,0:T(8,128)(2,1)S(1)}, bf16[64,1024]{1,0:T(8,128)(2,1)S(1)}, u32[]{:S(2)}, u32[]{:S(2)}) collective-permute-start(bf16[64,1024]{1,0:T(8,128)(2,1)S(1)} %get-tuple-element.75), channel_id=1, source_target_pairs={{0,1},{1,2},{2,3},{3,0},{4,5},{5,6},{6,7},{7,4},{8,9},{9,10},{10,1... | collective-permute-start | bytes 393224 | tf_op jit(solution)/shard_map/ppermute | solution.py:62
  33.0 1.7 %collective-permute-start.12 = (bf16[64,1024]{1,0:T(8,128)(2,1)S(1)}, bf16[64,1024]{1,0:T(8,128)(2,1)S(1)}, u32[]{:S(2)}, u32[]{:S(2)}) collective-permute-start(bf16[64,1024]{1,0:T(8,128)(2,1)S(1)} %get-tuple-element.76), channel_id=1, source_target_pairs={{0,2},{1,3},{2,0},{3,1},{4,6},{5,7},{6,4},{7,5},{8,10},{9,11},{10,... | collective-permute-start | bytes 393224 | tf_op jit(solution)/shard_map/ppermute | solution.py:62
  34.8 0.4 collective-permute-start.13
  35.3 1.9 %make_weights.1 = (bf16[1088,256]{1,0:T(8,128)(2,1)S(1)}, bf16[48,256]{1,0:T(8,128)(2,1)S(1)}, bf16[128,320]{1,0:T(8,128)(2,1)S(1)}, bf16[128,128]{1,0:T(8,128)(2,1)S(1)}) custom-call(f32[4]{0:T(128)S(1)} %copy-done, s32[4]{0:T(128)S(1)} %bitcast.11, bf16[16,9]{1,0:T(8,128)(2,1)S(1)} %copy.13.first_ref, bf16[9,16]{1,0:T(8,128)(2,1)S(1)} %bitcast.10), custom_call_target="tpu_custom_call" | custom-call | tf_op jit(solution)/shard_map/make_weights/pallas_call | solution.py:344
  37.2 0.6 %collective-permute-done.10.refs_0_ = bf16[64,1024]{1,0:T(8,128)(2,1)S(1)} collective-permute-done((bf16[64,1024]{1,0:T(8,128)(2,1)S(1)}, bf16[64,1024]{1,0:T(8,128)(2,1)S(1)}, u32[]{:S(2)}, u32[]{:S(2)}) %collective-permute-start.10) | collective-permute-done | bytes 131104 | tf_op jit(solution)/shard_map/ppermute | solution.py:499
  37.7 2.0 %collective-permute-done.11.refs_2_ = bf16[64,1024]{1,0:T(8,128)(2,1)S(1)} collective-permute-done((bf16[64,1024]{1,0:T(8,128)(2,1)S(1)}, bf16[64,1024]{1,0:T(8,128)(2,1)S(1)}, u32[]{:S(2)}, u32[]{:S(2)}) %collective-permute-start.11) | collective-permute-done | bytes 131104 | tf_op jit(solution)/shard_map/ppermute | solution.py:62
  39.8 0.8 %collective-permute-done.13.refs_4_ = bf16[64,1024]{1,0:T(8,128)(2,1)S(1)} collective-permute-done((bf16[64,1024]{1,0:T(8,128)(2,1)S(1)}, bf16[64,1024]{1,0:T(8,128)(2,1)S(1)}, u32[]{:S(2)}, u32[]{:S(2)}) %collective-permute-start.13) | collective-permute-done | bytes 131104 | tf_op jit(solution)/shard_map/ppermute | solution.py:62
  40.6 0.3 cut_slabs.1
  41.0 1.6 %collective-permute-start.15 = (bf16[32,1024]{1,0:T(8,128)(2,1)S(1)}, bf16[32,1024]{1,0:T(8,128)(2,1)S(1)}, u32[]{:S(2)}, u32[]{:S(2)}) collective-permute-start(bf16[32,1024]{1,0:T(8,128)(2,1)S(1)} %get-tuple-element.80), channel_id=1, source_target_pairs={{0,16},{8,24},{16,0},{24,8},{1,17},{9,25},{17,1},{25,9},{2,18},{10... | collective-permute-start | bytes 196616 | tf_op jit(solution)/shard_map/ppermute | solution.py:62
  42.6 1.4 %collective-permute-start.16 = (bf16[32,1024]{1,0:T(8,128)(2,1)S(1)}, bf16[32,1024]{1,0:T(8,128)(2,1)S(1)}, u32[]{:S(2)}, u32[]{:S(2)}) collective-permute-start(bf16[32,1024]{1,0:T(8,128)(2,1)S(1)} %get-tuple-element.81), channel_id=1, source_target_pairs={{0,24},{8,0},{16,8},{24,16},{1,25},{9,1},{17,9},{25,17},{2,26},{10... | collective-permute-start | bytes 196616 | tf_op jit(solution)/shard_map/ppermute | solution.py:62
  43.9 0.8 %collective-permute-done.14.refs_1_ = bf16[32,1024]{1,0:T(8,128)(2,1)S(1)} collective-permute-done((bf16[32,1024]{1,0:T(8,128)(2,1)S(1)}, bf16[32,1024]{1,0:T(8,128)(2,1)S(1)}, u32[]{:S(2)}, u32[]{:S(2)}) %collective-permute-start.14) | collective-permute-done | bytes 65568 | tf_op jit(solution)/shard_map/ppermute | solution.py:62
  44.7 0.8 %collective-permute-done.15.refs_2_ = bf16[32,1024]{1,0:T(8,128)(2,1)S(1)} collective-permute-done((bf16[32,1024]{1,0:T(8,128)(2,1)S(1)}, bf16[32,1024]{1,0:T(8,128)(2,1)S(1)}, u32[]{:S(2)}, u32[]{:S(2)}) %collective-permute-start.15) | collective-permute-done | bytes 65568 | tf_op jit(solution)/shard_map/ppermute | solution.py:62
  45.6 0.3 collective-permute-done.16.refs_3_
  45.8 9.4 %make_volume.1 = f32[32,16,1024]{2,1,0:T(8,128)} custom-call(bf16[32,1024]{1,0:T(8,128)(2,1)S(1)} %get-tuple-element.78.refs_0_, bf16[32,1024]{1,0:T(8,128)(2,1)S(1)} %collective-permute-done.14.refs_1_, bf16[32,1024]{1,0:T(8,128)(2,1)S(1)} %collective-permute-done.15.refs_2_, bf16[32,1024]{1,0:T(8,128)(2,1)S(1)} %collective-permute-done.16.refs_3_, ...), custom_call_target="tpu_custom_call" | custom-call | tf_op jit(solution)/shard_map/make_volume/pallas_call | solution.py:452
  (21 shorter events, 0.4 us)
Async XLA Ops:
  1.5 8.8 %collective-permute-start = (bf16[2,128,128]{2,1,0:T(8,128)(2,1)S(1)}, bf16[2,128,128]{2,1,0:T(8,128)(2,1)S(1)}, u32[]{:S(2)}, u32[]{:S(2)}) collective-permute-start(bf16[2,128,128]{2,1,0:T(8,128)(2,1)S(1)} %get-tuple-element.46), channel_id=1, source_target_pairs={{0,1},{1,2},{2,3},{3,4},{4,5},{5,6},{6,7},{7,0},{8,9},{9,10},{10,1... | collective-permute-start | bytes 196616 | tf_op jit(solution)/shard_map/ppermute | solution.py:62
  4.5 9.4 %collective-permute-start.1 = (bf16[2,128,128]{2,1,0:T(8,128)(2,1)S(1)}, bf16[2,128,128]{2,1,0:T(8,128)(2,1)S(1)}, u32[]{:S(2)}, u32[]{:S(2)}) collective-permute-start(bf16[2,128,128]{2,1,0:T(8,128)(2,1)S(1)} %get-tuple-element.47), channel_id=1, source_target_pairs={{0,7},{1,0},{2,1},{3,2},{4,3},{5,4},{6,5},{7,6},{8,15},{9,8},{10,9... | collective-permute-start | bytes 196616 | tf_op jit(solution)/shard_map/ppermute | solution.py:62
  7.6 9.1 %collective-permute-start.2 = (bf16[2,128,128]{2,1,0:T(8,128)(2,1)S(1)}, bf16[2,128,128]{2,1,0:T(8,128)(2,1)S(1)}, u32[]{:S(2)}, u32[]{:S(2)}) collective-permute-start(bf16[2,128,128]{2,1,0:T(8,128)(2,1)S(1)} %get-tuple-element.53), channel_id=1, source_target_pairs={{0,2},{1,3},{2,4},{3,5},{4,6},{5,7},{6,0},{7,1},{8,10},{9,11},{10,... | collective-permute-start | bytes 196616 | tf_op jit(solution)/shard_map/ppermute | solution.py:62
  7.6 9.1 %collective-permute-start.3 = (bf16[2,128,128]{2,1,0:T(8,128)(2,1)S(1)}, bf16[2,128,128]{2,1,0:T(8,128)(2,1)S(1)}, u32[]{:S(2)}, u32[]{:S(2)}) collective-permute-start(bf16[2,128,128]{2,1,0:T(8,128)(2,1)S(1)} %get-tuple-element.54), channel_id=1, source_target_pairs={{0,3},{1,4},{2,5},{3,6},{4,7},{5,0},{6,1},{7,2},{8,11},{9,12},{10,... | collective-permute-start | bytes 196616 | tf_op jit(solution)/shard_map/ppermute | solution.py:62
  9.1 9.8 %collective-permute-start.4 = (bf16[2,128,128]{2,1,0:T(8,128)(2,1)S(1)}, bf16[2,128,128]{2,1,0:T(8,128)(2,1)S(1)}, u32[]{:S(2)}, u32[]{:S(2)}) collective-permute-start(bf16[2,128,128]{2,1,0:T(8,128)(2,1)S(1)} %get-tuple-element.55), channel_id=1, source_target_pairs={{0,4},{1,5},{2,6},{3,7},{4,0},{5,1},{6,2},{7,3},{8,12},{9,13},{10,... | collective-permute-start | bytes 196616 | tf_op jit(solution)/shard_map/ppermute | solution.py:62
  10.3 8.6 %collective-permute-start.5 = (bf16[2,128,128]{2,1,0:T(8,128)(2,1)S(1)}, bf16[2,128,128]{2,1,0:T(8,128)(2,1)S(1)}, u32[]{:S(2)}, u32[]{:S(2)}) collective-permute-start(bf16[2,128,128]{2,1,0:T(8,128)(2,1)S(1)} %get-tuple-element.56), channel_id=1, source_target_pairs={{0,5},{1,6},{2,7},{3,0},{4,1},{5,2},{6,3},{7,4},{8,13},{9,14},{10,... | collective-permute-start | bytes 196616 | tf_op jit(solution)/shard_map/ppermute | solution.py:62
  13.9 5.7 %collective-permute-start.6 = (bf16[2,128,128]{2,1,0:T(8,128)(2,1)S(1)}, bf16[2,128,128]{2,1,0:T(8,128)(2,1)S(1)}, u32[]{:S(2)}, u32[]{:S(2)}) collective-permute-start(bf16[2,128,128]{2,1,0:T(8,128)(2,1)S(1)} %get-tuple-element.57), channel_id=1, source_target_pairs={{0,6},{1,7},{2,0},{3,1},{4,2},{5,3},{6,4},{7,5},{8,14},{9,15},{10,... | collective-permute-start | bytes 196616 | tf_op jit(solution)/shard_map/ppermute | solution.py:62
  15.9 19.2 %copy-start.2 = (bf16[16,1,3,3]{0,3,2,1:T(4,128)(2,1)S(1)}, bf16[16,1,3,3]{0,3,2,1:T(4,128)(2,1)}, u32[]{:S(2)}) copy-start(bf16[16,1,3,3]{0,3,2,1:T(4,128)(2,1)} %param.19) | copy-start | bytes 868
  15.9 19.3 %copy-start.3 = (bf16[1,16,3,3]{1,3,2,0:T(4,128)(2,1)S(1)}, bf16[1,16,3,3]{1,3,2,0:T(4,128)(2,1)}, u32[]{:S(2)}) copy-start(bf16[1,16,3,3]{1,3,2,0:T(4,128)(2,1)} %param.20) | copy-start | bytes 868
  16.0 19.3 %copy-start = (f32[4]{0:T(128)S(1)}, f32[4]{0:T(128)}, u32[]{:S(2)}) copy-start(f32[4]{0:T(128)} %tan_ref) | copy-start | bytes 52
  16.0 19.3 %copy-start.1 = (s32[1,4]{1,0:T(1,128)S(1)}, s32[1,4]{1,0:T(1,128)}, u32[]{:S(2)}) copy-start(s32[1,4]{1,0:T(1,128)} %param.17) | copy-start | bytes 52
  21.1 6.9 %collective-permute-start.7 = (bf16[64,1024]{1,0:T(8,128)(2,1)S(1)}, bf16[64,1024]{1,0:T(8,128)(2,1)S(1)}, u32[]{:S(2)}, u32[]{:S(2)}) collective-permute-start(bf16[64,1024]{1,0:T(8,128)(2,1)S(1)} %get-tuple-element.65), channel_id=1, source_target_pairs={{0,1},{1,2},{2,3},{3,0},{4,5},{5,6},{6,7},{7,4},{8,9},{9,10},{10,1... | collective-permute-start | bytes 393224 | tf_op jit(solution)/shard_map/ppermute | solution.py:62
  23.3 5.6 %collective-permute-start.8 = (bf16[64,1024]{1,0:T(8,128)(2,1)S(1)}, bf16[64,1024]{1,0:T(8,128)(2,1)S(1)}, u32[]{:S(2)}, u32[]{:S(2)}) collective-permute-start(bf16[64,1024]{1,0:T(8,128)(2,1)S(1)} %get-tuple-element.66), channel_id=1, source_target_pairs={{0,2},{1,3},{2,0},{3,1},{4,6},{5,7},{6,4},{7,5},{8,10},{9,11},{10,... | collective-permute-start | bytes 393224 | tf_op jit(solution)/shard_map/ppermute | solution.py:62
  23.4 6.1 %collective-permute-start.9 = (bf16[64,1024]{1,0:T(8,128)(2,1)S(1)}, bf16[64,1024]{1,0:T(8,128)(2,1)S(1)}, u32[]{:S(2)}, u32[]{:S(2)}) collective-permute-start(bf16[64,1024]{1,0:T(8,128)(2,1)S(1)} %get-tuple-element.67), channel_id=1, source_target_pairs={{0,3},{1,0},{2,1},{3,2},{4,7},{5,4},{6,5},{7,6},{8,11},{9,8},{10,9... | collective-permute-start | bytes 393224 | tf_op jit(solution)/shard_map/ppermute | solution.py:62
  29.6 8.1 %collective-permute-start.10 = (bf16[64,1024]{1,0:T(8,128)(2,1)S(1)}, bf16[64,1024]{1,0:T(8,128)(2,1)S(1)}, u32[]{:S(2)}, u32[]{:S(2)}) collective-permute-start(bf16[64,1024]{1,0:T(8,128)(2,1)S(1)} %add_convert_fusion), channel_id=1, source_target_pairs={{0,4},{1,5},{2,6},{3,7},{4,0},{5,1},{6,2},{7,3},{8,12},{9,13},{10,... | collective-permute-start | bytes 393224 | tf_op jit(solution)/shard_map/ppermute | solution.py:499
  31.6 8.2 %collective-permute-start.11 = (bf16[64,1024]{1,0:T(8,128)(2,1)S(1)}, bf16[64,1024]{1,0:T(8,128)(2,1)S(1)}, u32[]{:S(2)}, u32[]{:S(2)}) collective-permute-start(bf16[64,1024]{1,0:T(8,128)(2,1)S(1)} %get-tuple-element.75), channel_id=1, source_target_pairs={{0,1},{1,2},{2,3},{3,0},{4,5},{5,6},{6,7},{7,4},{8,9},{9,10},{10,1... | collective-permute-start | bytes 393224 | tf_op jit(solution)/shard_map/ppermute | solution.py:62
  33.0 6.7 %collective-permute-start.12 = (bf16[64,1024]{1,0:T(8,128)(2,1)S(1)}, bf16[64,1024]{1,0:T(8,128)(2,1)S(1)}, u32[]{:S(2)}, u32[]{:S(2)}) collective-permute-start(bf16[64,1024]{1,0:T(8,128)(2,1)S(1)} %get-tuple-element.76), channel_id=1, source_target_pairs={{0,2},{1,3},{2,0},{3,1},{4,6},{5,7},{6,4},{7,5},{8,10},{9,11},{10,... | collective-permute-start | bytes 393224 | tf_op jit(solution)/shard_map/ppermute | solution.py:62
  34.8 5.8 %collective-permute-start.13 = (bf16[64,1024]{1,0:T(8,128)(2,1)S(1)}, bf16[64,1024]{1,0:T(8,128)(2,1)S(1)}, u32[]{:S(2)}, u32[]{:S(2)}) collective-permute-start(bf16[64,1024]{1,0:T(8,128)(2,1)S(1)} %get-tuple-element.77), channel_id=1, source_target_pairs={{0,3},{1,0},{2,1},{3,2},{4,7},{5,4},{6,5},{7,6},{8,11},{9,8},{10,9... | collective-permute-start | bytes 393224 | tf_op jit(solution)/shard_map/ppermute | solution.py:62
  40.9 3.8 %collective-permute-start.14 = (bf16[32,1024]{1,0:T(8,128)(2,1)S(1)}, bf16[32,1024]{1,0:T(8,128)(2,1)S(1)}, u32[]{:S(2)}, u32[]{:S(2)}) collective-permute-start(bf16[32,1024]{1,0:T(8,128)(2,1)S(1)} %get-tuple-element.79), channel_id=1, source_target_pairs={{0,8},{8,16},{16,24},{24,0},{1,9},{9,17},{17,25},{25,1},{2,10},{10... | collective-permute-start | bytes 196616 | tf_op jit(solution)/shard_map/ppermute | solution.py:62
  41.0 4.6 %collective-permute-start.15 = (bf16[32,1024]{1,0:T(8,128)(2,1)S(1)}, bf16[32,1024]{1,0:T(8,128)(2,1)S(1)}, u32[]{:S(2)}, u32[]{:S(2)}) collective-permute-start(bf16[32,1024]{1,0:T(8,128)(2,1)S(1)} %get-tuple-element.80), channel_id=1, source_target_pairs={{0,16},{8,24},{16,0},{24,8},{1,17},{9,25},{17,1},{25,9},{2,18},{10... | collective-permute-start | bytes 196616 | tf_op jit(solution)/shard_map/ppermute | solution.py:62
  42.6 3.3 %collective-permute-start.16 = (bf16[32,1024]{1,0:T(8,128)(2,1)S(1)}, bf16[32,1024]{1,0:T(8,128)(2,1)S(1)}, u32[]{:S(2)}, u32[]{:S(2)}) collective-permute-start(bf16[32,1024]{1,0:T(8,128)(2,1)S(1)} %get-tuple-element.81), channel_id=1, source_target_pairs={{0,24},{8,0},{16,8},{24,16},{1,25},{9,1},{17,9},{25,17},{2,26},{10... | collective-permute-start | bytes 196616 | tf_op jit(solution)/shard_map/ppermute | solution.py:62
